TPU v7x, 32 devices: a whole 2x2x4 slice. The times are simulated.
32 devices in a mesh: phase: 2 (over x), ctx: 4 (over z), head: 4 (over y, core).
Axes of the slice: x: 2, y: 2, z: 4, core: 2. Of those that a mesh axis runs over, the one named last changes fastest.
Arguments:
- query: bfloat16 [2, 1024, 5120], P('phase', 'ctx', 'head'), may hold values from -18 to 18
- key_cache: bfloat16 [1024, 1024], P('ctx', 'head'), may hold values from -18 to 18
- value_cache: bfloat16 [1024, 1024], P('ctx', 'head'), may hold values from -6 to 6
- saved_output: bfloat16 [2, 1024, 5120], P('phase', 'ctx', 'head'), may hold values from -1.796875 to 1.796875
- out_grad: bfloat16 [2, 1024, 5120], P('phase', 'ctx', 'head'), may hold values from -6 to 6
- out_weight: bfloat16 [2, 5120, 5120], P('phase', 'head'), may hold values from -0.078125 to 0.078125
- doc_lengths: int32 [4], replicated, may hold values from 1 to 768, 1024 in all
Outputs:
- grad_query: float32 [2, 1024, 5120], P('phase', 'ctx', 'head')
- grad_key: float32 [1024, 1024], P('ctx', 'head')
- grad_value: float32 [1024, 1024], P('ctx', 'head')
Inputs may be any that keep to these rules, and one draw needn't show every extreme that they name: `doc_lengths`: the 4 lengths sum to 1024, and one document has exactly 768 positions.
All inputs are finite; a program needn't handle non-finite values.
Results may differ from a plain program's by a relative error of at most 0.0041.
Values may be sent and summed in bfloat16 or wider, within the bound.
A program may use at most 128 MiB of HBM per device.

v0:
```python
import functools
import math

import jax
import jax.numpy as jnp
from jax import lax
from jax.experimental import pallas as pl
from jax.experimental.pallas import tpu as pltpu
from jax.sharding import PartitionSpec as P

HD = 128
MASKED = -1e30
LAG = 2
MESH = pl.DeviceIdType.MESH


def nt(a, b):
    return lax.dot_general(a, b, (((1,), (1,)), ((), ())), preferred_element_type=jnp.float32)


def nn(a, b):
    return jnp.dot(a, b, preferred_element_type=jnp.float32)


def kernel(
    sizes,
    query_ref, key_ref, value_ref, saved_ref, grad_ref, weight_ref, doc_ref,
    dq_ref, dk_ref, dv_ref,
    wbuf, qbuf, obuf, kall, vall, psend, precv, ysend, yrecv, own, qs, gs, prob, bias, inv, delta,
    plow, dlow, dqt, xsend, xrecv, keep, zsend, zrecv, fsend, frecv,
    w_sem, in_sem, kv_s, kv_r, fw_s, fw_r, p_s, p_r, y_s, y_r, x_s, x_r, z_s, z_r, f_s, f_r,
):
    n, nh, rows, kvh, groups, docs, subs = sizes
    ys = nh // 2
    feats = kvh * groups * HD
    sw = feats // subs
    half = rows // 2
    scale = HD ** (-0.5)
    phase = lax.axis_index("phase")
    rank = lax.axis_index("ctx")
    head = lax.axis_index("head")
    y, core = head // 2, lax.rem(head, 2)
    other = 1 - phase
    partner = head + 1 - 2 * core
    mine = pl.ds(pl.multiple_of(phase * half, half), half)

    order = [dy for dy in range(1, ys)] + [0]
    loads = {}

    def load(dy, which, s):
        i = (dy * 2 + which) * subs + s
        dest = lax.rem(y + dy, ys) * 2 + (1 - core if which == 0 else core)
        at = pl.multiple_of(dest * feats + s * sw, HD)
        return pltpu.make_async_copy(weight_ref.at[:, pl.ds(at, sw)], wbuf.at[i], w_sem.at[i])

    def schedule():
        for dy in order:
            for t in range(subs + LAG):
                if t < subs:
                    yield dy, 0, t
                if t >= LAG:
                    yield dy, 1, t - LAG

    for step in schedule():
        loads[step] = load(*step)
        loads[step].start()
    query_copy = pltpu.make_async_copy(query_ref.at[0], qbuf, in_sem.at[0])
    saved_copy = pltpu.make_async_copy(saved_ref.at[0], obuf, in_sem.at[1])
    query_copy.start()
    saved_copy.start()

    barrier = pltpu.get_barrier_semaphore()
    pl.semaphore_signal(barrier, inc=1, device_id={"phase": other}, device_id_type=MESH)
    pl.semaphore_signal(barrier, inc=1, device_id={"head": partner}, device_id_type=MESH)
    for dy in range(1, ys):
        there = lax.rem(y + dy, ys) * 2 + core
        pl.semaphore_signal(barrier, inc=1, device_id={"head": there}, device_id_type=MESH)
    for d in range(1, n):
        pl.semaphore_signal(barrier, inc=1, device_id={"ctx": lax.rem(rank + d, n)}, device_id_type=MESH)
    pl.semaphore_wait(barrier, 2 + (ys - 1) + (n - 1))

    def kv_copy(which, d):
        src, dst = ((key_ref, kall), (value_ref, vall))[which]
        return pltpu.make_async_remote_copy(
            src_ref=src.at[mine], dst_ref=dst.at[rank, mine],
            send_sem=kv_s.at[which, d], recv_sem=kv_r.at[which, d],
            device_id={"ctx": rank + d}, device_id_type=MESH,
        )

    def kv_arrival(which, d):
        dst = (kall, vall)[which].at[rank - d, mine]
        return pltpu.make_async_remote_copy(
            src_ref=dst, dst_ref=dst,
            send_sem=fw_s.at[which, d], recv_sem=kv_r.at[which, d],
            device_id={"phase": other}, device_id_type=MESH,
        )

    def forward(which, d):
        dst = (kall, vall)[which].at[rank - d, mine]
        return pltpu.make_async_remote_copy(
            src_ref=dst, dst_ref=dst,
            send_sem=fw_s.at[which, d], recv_sem=fw_r.at[which, d],
            device_id={"phase": other}, device_id_type=MESH,
        )

    for which in range(2):
        @pl.loop(1, n - rank)
        def _(d):
            kv_copy(which, d).start()

    kall[rank] = key_ref[...]
    vall[rank] = value_ref[...]

    def to_partner(dy, s):
        i = dy * subs + s
        return pltpu.make_async_remote_copy(
            src_ref=psend.at[i], dst_ref=precv.at[i], send_sem=p_s.at[i], recv_sem=p_r.at[i],
            device_id={"head": partner}, device_id_type=MESH,
        )

    def to_chip(dy, s):
        i = (dy - 1) * subs + s
        return pltpu.make_async_remote_copy(
            src_ref=ysend.at[i], dst_ref=yrecv.at[i], send_sem=y_s.at[i], recv_sem=y_r.at[i],
            device_id={"head": lax.rem(y + dy, ys) * 2 + core}, device_id_type=MESH,
        )

    for dy, which, s in schedule():
        loads[dy, which, s].wait()
        part = nn(grad_ref[0], wbuf[(dy * 2 + which) * subs + s])
        if which == 0:
            psend[dy * subs + s] = part
            to_partner(dy, s).start()
        else:
            to_partner(dy, s).wait_recv()
            part = part + precv[dy * subs + s]
            if dy:
                ysend[(dy - 1) * subs + s] = part.astype(jnp.bfloat16)
                to_chip(dy, s).start()
            else:
                own[s] = part

    query_copy.wait()
    for j in range(kvh):
        for g in range(groups):
            qs[j, g * rows:(g + 1) * rows] = qbuf[:, (j * groups + g) * HD:(j * groups + g + 1) * HD]
    query_place = rank * rows + lax.broadcasted_iota(jnp.int32, (1, rows), 1)
    begin = jnp.zeros((1, rows), jnp.int32)
    end = jnp.int32(0)
    for d in range(docs):
        end = end + doc_ref[d]
        begin = jnp.where(query_place >= end, jnp.maximum(begin, end), begin)

    @pl.loop(0, rank + 1)
    def _(b):
        place = b * rows + lax.broadcasted_iota(jnp.int32, (rows, rows), 0)
        bias[b] = jnp.where((place <= query_place) & (place >= begin), 0.0, MASKED)

    @pl.loop(1, rank + 1)
    def _(d):
        kv_arrival(0, d).wait_recv()
        forward(0, d).start()

    @pl.loop(1, rank + 1)
    def _(d):
        kv_arrival(1, d).wait_recv()
        forward(1, d).start()

    def forwarded(which, d):
        dst = (kall, vall)[which].at[rank - d, pl.ds(pl.multiple_of(other * half, half), half)]
        return pltpu.make_async_remote_copy(
            src_ref=dst, dst_ref=dst, send_sem=fw_s.at[which, d], recv_sem=fw_r.at[which, d],
            device_id={"phase": other}, device_id_type=MESH,
        )

    @pl.loop(1, rank + 1)
    def _(d):
        forwarded(0, d).wait_recv()

    factor = scale * math.log2(math.e)
    for j in range(kvh):
        cols = slice(j * HD, (j + 1) * HD)

        def score_step(b, largest):
            raised = []
            keys = kall[b, :, cols]
            for g in range(groups):
                span = slice(g * rows, (g + 1) * rows)
                s = nt(keys, qs[j, span]) * factor + bias[b]
                prob[j, b, :, span] = s
                raised.append(jnp.maximum(largest[g], jnp.max(s, axis=0, keepdims=True)))
            return tuple(raised)

        largest = lax.fori_loop(
            0, rank + 1, score_step, (jnp.full((1, rows), MASKED, jnp.float32),) * groups
        )

        def exp_step(b, total):
            sums = []
            for g in range(groups):
                span = slice(g * rows, (g + 1) * rows)
                e = jnp.exp2(prob[j, b, :, span] - largest[g])
                prob[j, b, :, span] = e
                sums.append(total[g] + jnp.sum(e, axis=0, keepdims=True))
            return tuple(sums)

        total = lax.fori_loop(
            0, rank + 1, exp_step, (jnp.zeros((1, rows), jnp.float32),) * groups
        )
        for g in range(groups):
            inv[j, :, g * rows:(g + 1) * rows] = jnp.broadcast_to(1.0 / total[g], (8, rows))

    saved_copy.wait()
    ones = jnp.ones((8, HD), jnp.bfloat16)
    for s in range(subs):
        part = own[s]
        for dy in range(1, ys):
            to_chip(dy, s).wait_recv()
            part = part + yrecv[(dy - 1) * subs + s].astype(jnp.float32)
        low = part.astype(jnp.bfloat16)
        for at in range(0, sw, HD):
            h = (s * sw + at) // HD
            j, g = h // groups, h % groups
            span = slice(g * rows, (g + 1) * rows)
            one = low[:, at:at + HD]
            gs[j, span] = one
            both = one.astype(jnp.float32) * obuf[:, h * HD:(h + 1) * HD].astype(jnp.float32)
            high = both.astype(jnp.bfloat16)
            rest = (both - high.astype(jnp.float32)).astype(jnp.bfloat16)
            delta[j, :, span] = nt(ones, high) + nt(ones, rest)

    @pl.loop(1, rank + 1)
    def _(d):
        forwarded(1, d).wait_recv()

    def to_phase(j, b):
        return pltpu.make_async_remote_copy(
            src_ref=xsend.at[j, b], dst_ref=xrecv.at[j, b], send_sem=x_s.at[j, b], recv_sem=x_r.at[j, b],
            device_id={"phase": other}, device_id_type=MESH,
        )

    def to_owner(j, b):
        return pltpu.make_async_remote_copy(
            src_ref=zsend.at[j, b], dst_ref=zrecv.at[j, rank - b],
            send_sem=z_s.at[j, rank - b], recv_sem=z_r.at[j, rank - b],
            device_id={"ctx": b}, device_id_type=MESH,
        )

    def from_later(j, d):
        return pltpu.make_async_remote_copy(
            src_ref=zsend.at[j, 0], dst_ref=zrecv.at[j, d], send_sem=z_s.at[j, d], recv_sem=z_r.at[j, d],
            device_id={"ctx": lax.rem(rank + d, n)}, device_id_type=MESH,
        )

    def send_on(j, b):
        to_phase(j, b).wait_recv()
        zsend[j, b] = (keep[j, b] + xrecv[j, b].astype(jnp.float32)).astype(jnp.bfloat16)
        to_owner(j, b).start()

    for j in range(kvh):
        cols = slice(j * HD, (j + 1) * HD)
        dqt[...] = jnp.zeros_like(dqt)

        @pl.loop(0, rank + 1)
        def _(b):
            values = vall[b, :, cols]
            for g in range(groups):
                span = slice(g * rows, (g + 1) * rows)
                p = prob[j, b, :, span] * inv[j, 0:1, span]
                plow[:, span] = p.astype(jnp.bfloat16)
                wide = nt(values, gs[j, span])
                dlow[:, span] = (p * (wide - delta[j, 0:1, span])).astype(jnp.bfloat16)
            dv = nn(plow[...], gs[j])
            dk = nn(dlow[...], qs[j]) * scale
            keep[j, b] = jnp.where(phase == 0, dk, dv)
            xsend[j, b] = jnp.where(phase == 0, dv, dk).astype(jnp.bfloat16)
            to_phase(j, b).start()
            turned = kall[b, :, cols].astype(jnp.float32).T.astype(jnp.bfloat16)
            dqt[...] += nn(turned, dlow[...])
            if j:
                @pl.when(b < rank)
                def _():
                    send_on(j - 1, b)

        for g in range(groups):
            h = j * groups + g
            dq_ref[0, :, h * HD:(h + 1) * HD] = dqt[:, g * rows:(g + 1) * rows].T * scale

    @pl.loop(0, rank)
    def _(b):
        send_on(kvh - 1, b)

    for j in range(kvh):
        cols = slice(j * HD, (j + 1) * HD)
        to_phase(j, rank).wait_recv()
        fsend[:, cols] = keep[j, rank] + xrecv[j, rank].astype(jnp.float32)

        @pl.loop(1, n - rank)
        def _(d):
            from_later(j, d).wait_recv()
            fsend[:, cols] += zrecv[j, d].astype(jnp.float32)

    last = pltpu.make_async_remote_copy(
        src_ref=fsend, dst_ref=frecv, send_sem=f_s, recv_sem=f_r,
        device_id={"phase": other}, device_id_type=MESH,
    )
    last.start()

    for which in range(2):
        @pl.loop(1, n - rank)
        def _(d):
            kv_copy(which, d).wait_send()

        @pl.loop(1, rank + 1)
        def _(d):
            forward(which, d).wait_send()

    for dy in range(ys):
        for s in range(subs):
            to_partner(dy, s).wait_send()
            if dy:
                to_chip(dy, s).wait_send()
    for j in range(kvh):
        @pl.loop(0, rank + 1)
        def _(b):
            to_phase(j, b).wait_send()

        @pl.loop(0, rank)
        def _(b):
            to_owner(j, b).wait_send()

    last.wait()
    dk_ref[...] = jnp.where(phase == 0, fsend[...], frecv[...])
    dv_ref[...] = jnp.where(phase == 0, frecv[...], fsend[...])


def body(n, nh, query, key_cache, value_cache, saved_output, out_grad, out_weight, doc_lengths):
    rows, feats = query.shape[1:]
    width, kc = out_weight.shape[1], key_cache.shape[1]
    kvh = kc // HD
    groups = feats // kc
    ys, subs = nh // 2, groups
    sw = feats // subs
    bf, f32 = jnp.bfloat16, jnp.float32
    vmem = pltpu.VMEM
    dma = pltpu.SemaphoreType.DMA
    others = max(ys - 1, 1) * subs
    stack = groups * rows
    full = pl.BlockSpec(memory_space=pltpu.VMEM)
    anywhere = pl.BlockSpec(memory_space=pl.ANY)
    sizes = (n, nh, rows, kvh, groups, doc_lengths.shape[0], subs)
    return pl.pallas_call(
        functools.partial(kernel, sizes),
        out_shape=(
            jax.ShapeDtypeStruct((1, rows, feats), f32),
            jax.ShapeDtypeStruct((rows, kc), f32),
            jax.ShapeDtypeStruct((rows, kc), f32),
        ),
        in_specs=[anywhere, full, full, anywhere, full, anywhere, pl.BlockSpec(memory_space=pltpu.SMEM)],
        out_specs=(full, full, full),
        scratch_shapes=[
            vmem((2 * ys * subs, width, sw), bf),
            vmem((rows, feats), bf),
            vmem((rows, feats), bf),
            vmem((n, rows, kc), bf),
            vmem((n, rows, kc), bf),
            vmem((ys * subs, rows, sw), f32),
            vmem((ys * subs, rows, sw), f32),
            vmem((others, rows, sw), bf),
            vmem((others, rows, sw), bf),
            vmem((subs, rows, sw), f32),
            vmem((kvh, stack, HD), bf),
            vmem((kvh, stack, HD), bf),
            vmem((kvh, n, rows, stack), f32),
            vmem((n, rows, rows), f32),
            vmem((kvh, 8, stack), f32),
            vmem((kvh, 8, stack), f32),
            vmem((rows, stack), bf),
            vmem((rows, stack), bf),
            vmem((HD, stack), f32),
            vmem((kvh, n, rows, HD), bf),
            vmem((kvh, n, rows, HD), bf),
            vmem((kvh, n, rows, HD), f32),
            vmem((kvh, n, rows, HD), bf),
            vmem((kvh, n, rows, HD), bf),
            vmem((rows, kc), f32),
            vmem((rows, kc), f32),
            dma((2 * ys * subs,)),
            dma((2,)),
            dma((2, n)), dma((2, n)), dma((2, n)), dma((2, n)),
            dma((ys * subs,)), dma((ys * subs,)),
            dma((others,)), dma((others,)),
            dma((kvh, n)), dma((kvh, n)), dma((kvh, n)), dma((kvh, n)),
            dma(()), dma(()),
        ],
        compiler_params=pltpu.CompilerParams(
            collective_id=0, has_side_effects=True, vmem_limit_bytes=60 * 2**20
        ),
        name="fused",
    )(query, key_cache, value_cache, saved_output, out_grad, out_weight[0], doc_lengths)


def solution(mesh):
    placed = (
        P("phase", "ctx", "head"),
        P("ctx", "head"),
        P("ctx", "head"),
        P("phase", "ctx", "head"),
        P("phase", "ctx", "head"),
        P("phase", "head", None),
        P(),
    )
    return jax.shard_map(
        functools.partial(body, mesh.shape["ctx"], mesh.shape["head"]),
        mesh=mesh,
        in_specs=placed,
        out_specs=(P("phase", "ctx", "head"), P("ctx", "head"), P("ctx", "head")),
        check_vma=False,
    )
```

profile of v0, /device:TPU:0, one launch (start us, length us, event | category | flops | bytes accessed | tf_op | source)
XLA Modules:
  0.0 57.5 jit_solution(4024436936175602413)
XLA Ops:
  0.6 52.9 %fused.1 = (f32[1,256,1280]{2,1,0:T(8,128)}, f32[256,256]{1,0:T(8,128)}, f32[256,256]{1,0:T(8,128)}) custom-call(bf16[1,256,1280]{2,1,0:T(8,128)(2,1)} %query_ref.1, bf16[256,256]{1,0:T(8,128)(2,1)} %key_ref.1, bf16[256,256]{1,0:T(8,128)(2,1)} %value_ref.1, bf16[1,256,1280]{2,1,0:T(8,128)(2,1)} %saved_ref.1, bf16[1,256,1280]{2,1,0:T(8,128)(2,1)} %grad_ref.1, ...), custom_call_target="tpu_custom_call" | custom-call | tf_op jit(solution)/shard_map/fused/pallas_call | solution.py:352
  53.5 0.0 copy-start.1
  53.5 0.0 copy-start
  53.5 2.5 %copy.13 = f32[1,256,1280]{2,1,0:T(8,128)} copy(f32[1,256,1280]{2,1,0:T(8,128)} %get-tuple-element.6) | data formatting | bytes 2621440
  56.1 0.0 copy-done.1
  56.1 0.7 %copy.14 = f32[256,256]{1,0:T(8,128)} copy(f32[256,256]{1,0:T(8,128)S(1)} %copy-done.1) | data formatting | bytes 524288
  56.8 0.0 copy-done
  56.8 0.7 %copy.15 = f32[256,256]{1,0:T(8,128)} copy(f32[256,256]{1,0:T(8,128)S(1)} %copy-done) | data formatting | bytes 524288
Async XLA Ops:
  53.5 2.5 %copy-start.1 = (f32[256,256]{1,0:T(8,128)S(1)}, f32[256,256]{1,0:T(8,128)}, u32[]{:S(2)}) copy-start(f32[256,256]{1,0:T(8,128)} %get-tuple-element.7) | copy-start | bytes 786436
  53.5 3.2 %copy-start = (f32[256,256]{1,0:T(8,128)S(1)}, f32[256,256]{1,0:T(8,128)}, u32[]{:S(2)}) copy-start(f32[256,256]{1,0:T(8,128)} %get-tuple-element.8) | copy-start | bytes 786436
where the time goes:
time: 57.6 us; the launch traced here: 57.5 us
  Pallas kernels  52.9 us (92%)
  local copies, waits for them, and re-layouts  3.93 us (7%)
  between operations  0.66 us (1%)
    pallas_call x1, Pallas kernels, body(): pl.pallas_call(functools.partial(kernel, sizes), out_shape=(jax.ShapeDtyp...  52.9 us
    unnamed x7, local copies, waits for them, and re-layouts  3.93 us

commit v1 on v0

--- a/solution.py
+++ b/solution.py
@@ -11,6 +11,7 @@
 HD = 128
 MASKED = -1e30
 LAG = 2
+AHEAD = 4
 MESH = pl.DeviceIdType.MESH
 
 
@@ -44,30 +45,21 @@
     partner = head + 1 - 2 * core
     mine = pl.ds(pl.multiple_of(phase * half, half), half)
 
-    order = [dy for dy in range(1, ys)] + [0]
-    loads = {}
-
-    def load(dy, which, s):
-        i = (dy * 2 + which) * subs + s
-        dest = lax.rem(y + dy, ys) * 2 + (1 - core if which == 0 else core)
-        at = pl.multiple_of(dest * feats + s * sw, HD)
+    count = ys * subs
+
+    def load(which, q):
+        dest = lax.rem(y + q // subs + 1, ys) * 2 + (1 - core if which == 0 else core)
+        at = pl.multiple_of(dest * feats + lax.rem(q, subs) * sw, HD)
+        i = which * count + q
         return pltpu.make_async_copy(weight_ref.at[:, pl.ds(at, sw)], wbuf.at[i], w_sem.at[i])
 
-    def schedule():
-        for dy in order:
-            for t in range(subs + LAG):
-                if t < subs:
-                    yield dy, 0, t
-                if t >= LAG:
-                    yield dy, 1, t - LAG
-
-    for step in schedule():
-        loads[step] = load(*step)
-        loads[step].start()
+    for t in range(AHEAD):
+        if t < count:
+            load(0, jnp.int32(t)).start()
+        if 0 <= t - LAG < count:
+            load(1, jnp.int32(t - LAG)).start()
     query_copy = pltpu.make_async_copy(query_ref.at[0], qbuf, in_sem.at[0])
     saved_copy = pltpu.make_async_copy(saved_ref.at[0], obuf, in_sem.at[1])
-    query_copy.start()
-    saved_copy.start()
 
     barrier = pltpu.get_barrier_semaphore()
     pl.semaphore_signal(barrier, inc=1, device_id={"phase": other}, device_id_type=MESH)
@@ -111,39 +103,64 @@
     kall[rank] = key_ref[...]
     vall[rank] = value_ref[...]
 
-    def to_partner(dy, s):
-        i = dy * subs + s
-        return pltpu.make_async_remote_copy(
-            src_ref=psend.at[i], dst_ref=precv.at[i], send_sem=p_s.at[i], recv_sem=p_r.at[i],
+    def to_partner(q):
+        return pltpu.make_async_remote_copy(
+            src_ref=psend.at[q], dst_ref=precv.at[q], send_sem=p_s.at[q], recv_sem=p_r.at[q],
             device_id={"head": partner}, device_id_type=MESH,
         )
 
-    def to_chip(dy, s):
-        i = (dy - 1) * subs + s
-        return pltpu.make_async_remote_copy(
-            src_ref=ysend.at[i], dst_ref=yrecv.at[i], send_sem=y_s.at[i], recv_sem=y_r.at[i],
-            device_id={"head": lax.rem(y + dy, ys) * 2 + core}, device_id_type=MESH,
-        )
-
-    for dy, which, s in schedule():
-        loads[dy, which, s].wait()
-        part = nn(grad_ref[0], wbuf[(dy * 2 + which) * subs + s])
-        if which == 0:
-            psend[dy * subs + s] = part
-            to_partner(dy, s).start()
-        else:
-            to_partner(dy, s).wait_recv()
-            part = part + precv[dy * subs + s]
-            if dy:
-                ysend[(dy - 1) * subs + s] = part.astype(jnp.bfloat16)
-                to_chip(dy, s).start()
-            else:
-                own[s] = part
+    def to_chip(q):
+        return pltpu.make_async_remote_copy(
+            src_ref=ysend.at[q], dst_ref=yrecv.at[q], send_sem=y_s.at[q], recv_sem=y_r.at[q],
+            device_id={"head": lax.rem(y + q // subs + 1, ys) * 2 + core}, device_id_type=MESH,
+        )
+
+    far = (ys - 1) * subs
+
+    @pl.loop(0, count + LAG)
+    def _(t):
+        @pl.when(t + AHEAD < count)
+        def _():
+            load(0, t + AHEAD).start()
+
+        @pl.when(t + AHEAD - LAG < count)
+        def _():
+            load(1, t + AHEAD - LAG).start()
+
+        @pl.when(t < count)
+        def _():
+            load(0, t).wait()
+            psend[t] = nn(grad_ref[0], wbuf[t])
+            to_partner(t).start()
+
+        @pl.when(t >= LAG)
+        def _():
+            q = t - LAG
+            load(1, q).wait()
+            part = nn(grad_ref[0], wbuf[count + q])
+            to_partner(q).wait_recv()
+            part = part + precv[q]
+
+            @pl.when(q < far)
+            def _():
+                ysend[q] = part.astype(jnp.bfloat16)
+                to_chip(q).start()
+
+            @pl.when(q >= far)
+            def _():
+                own[q - far] = part
+
+        @pl.when(t == count - AHEAD)
+        def _():
+            query_copy.start()
+            saved_copy.start()
 
     query_copy.wait()
-    for j in range(kvh):
-        for g in range(groups):
-            qs[j, g * rows:(g + 1) * rows] = qbuf[:, (j * groups + g) * HD:(j * groups + g + 1) * HD]
+    @pl.loop(0, kvh * groups)
+    def _(h):
+        span = pl.ds(pl.multiple_of(lax.rem(h, groups) * rows, rows), rows)
+        qs[h // groups, span] = qbuf[:, pl.ds(pl.multiple_of(h * HD, HD), HD)]
+
     query_place = rank * rows + lax.broadcasted_iota(jnp.int32, (1, rows), 1)
     begin = jnp.zeros((1, rows), jnp.int32)
     end = jnp.int32(0)
@@ -178,8 +195,9 @@
         forwarded(0, d).wait_recv()
 
     factor = scale * math.log2(math.e)
-    for j in range(kvh):
-        cols = slice(j * HD, (j + 1) * HD)
+    @pl.loop(0, kvh)
+    def _(j):
+        cols = pl.ds(pl.multiple_of(j * HD, HD), HD)
 
         def score_step(b, largest):
             raised = []
@@ -212,22 +230,23 @@
 
     saved_copy.wait()
     ones = jnp.ones((8, HD), jnp.bfloat16)
-    for s in range(subs):
+    @pl.loop(0, subs)
+    def _(s):
         part = own[s]
         for dy in range(1, ys):
-            to_chip(dy, s).wait_recv()
+            to_chip((dy - 1) * subs + s).wait_recv()
             part = part + yrecv[(dy - 1) * subs + s].astype(jnp.float32)
         low = part.astype(jnp.bfloat16)
-        for at in range(0, sw, HD):
-            h = (s * sw + at) // HD
-            j, g = h // groups, h % groups
-            span = slice(g * rows, (g + 1) * rows)
-            one = low[:, at:at + HD]
-            gs[j, span] = one
-            both = one.astype(jnp.float32) * obuf[:, h * HD:(h + 1) * HD].astype(jnp.float32)
+        for a in range(sw // HD):
+            h = s * (sw // HD) + a
+            span = pl.ds(pl.multiple_of(lax.rem(h, groups) * rows, rows), rows)
+            one = low[:, a * HD:(a + 1) * HD]
+            gs[h // groups, span] = one
+            saved = obuf[:, pl.ds(pl.multiple_of(h * HD, HD), HD)]
+            both = one.astype(jnp.float32) * saved.astype(jnp.float32)
             high = both.astype(jnp.bfloat16)
             rest = (both - high.astype(jnp.float32)).astype(jnp.bfloat16)
-            delta[j, :, span] = nt(ones, high) + nt(ones, rest)
+            delta[h // groups, :, span] = nt(ones, high) + nt(ones, rest)
 
     @pl.loop(1, rank + 1)
     def _(d):
@@ -257,8 +276,9 @@
         zsend[j, b] = (keep[j, b] + xrecv[j, b].astype(jnp.float32)).astype(jnp.bfloat16)
         to_owner(j, b).start()
 
-    for j in range(kvh):
-        cols = slice(j * HD, (j + 1) * HD)
+    @pl.loop(0, kvh)
+    def _(j):
+        cols = pl.ds(pl.multiple_of(j * HD, HD), HD)
         dqt[...] = jnp.zeros_like(dqt)
 
         @pl.loop(0, rank + 1)
@@ -277,34 +297,36 @@
             to_phase(j, b).start()
             turned = kall[b, :, cols].astype(jnp.float32).T.astype(jnp.bfloat16)
             dqt[...] += nn(turned, dlow[...])
-            if j:
-                @pl.when(b < rank)
-                def _():
-                    send_on(j - 1, b)
+
+            @pl.when((j > 0) & (b < rank))
+            def _():
+                send_on(j - 1, b)
 
         for g in range(groups):
-            h = j * groups + g
-            dq_ref[0, :, h * HD:(h + 1) * HD] = dqt[:, g * rows:(g + 1) * rows].T * scale
+            at = pl.ds(pl.multiple_of((j * groups + g) * HD, HD), HD)
+            dq_ref[0, :, at] = dqt[:, g * rows:(g + 1) * rows].T * scale
 
     @pl.loop(0, rank)
     def _(b):
         send_on(kvh - 1, b)
 
-    for j in range(kvh):
-        cols = slice(j * HD, (j + 1) * HD)
+    def last(j):
+        return pltpu.make_async_remote_copy(
+            src_ref=fsend.at[j], dst_ref=frecv.at[j], send_sem=f_s.at[j], recv_sem=f_r.at[j],
+            device_id={"phase": other}, device_id_type=MESH,
+        )
+
+    @pl.loop(0, kvh)
+    def _(j):
         to_phase(j, rank).wait_recv()
-        fsend[:, cols] = keep[j, rank] + xrecv[j, rank].astype(jnp.float32)
+        fsend[j] = keep[j, rank] + xrecv[j, rank].astype(jnp.float32)
 
         @pl.loop(1, n - rank)
         def _(d):
             from_later(j, d).wait_recv()
-            fsend[:, cols] += zrecv[j, d].astype(jnp.float32)
-
-    last = pltpu.make_async_remote_copy(
-        src_ref=fsend, dst_ref=frecv, send_sem=f_s, recv_sem=f_r,
-        device_id={"phase": other}, device_id_type=MESH,
-    )
-    last.start()
+            fsend[j] += zrecv[j, d].astype(jnp.float32)
+
+        last(j).start()
 
     for which in range(2):
         @pl.loop(1, n - rank)
@@ -315,12 +337,16 @@
         def _(d):
             forward(which, d).wait_send()
 
-    for dy in range(ys):
-        for s in range(subs):
-            to_partner(dy, s).wait_send()
-            if dy:
-                to_chip(dy, s).wait_send()
-    for j in range(kvh):
+    @pl.loop(0, count)
+    def _(q):
+        to_partner(q).wait_send()
+
+    @pl.loop(0, far)
+    def _(q):
+        to_chip(q).wait_send()
+
+    @pl.loop(0, kvh)
+    def _(j):
         @pl.loop(0, rank + 1)
         def _(b):
             to_phase(j, b).wait_send()
@@ -329,9 +355,11 @@
         def _(b):
             to_owner(j, b).wait_send()
 
-    last.wait()
-    dk_ref[...] = jnp.where(phase == 0, fsend[...], frecv[...])
-    dv_ref[...] = jnp.where(phase == 0, frecv[...], fsend[...])
+    for j in range(kvh):
+        last(j).wait()
+        cols = slice(j * HD, (j + 1) * HD)
+        dk_ref[:, cols] = jnp.where(phase == 0, fsend[j], frecv[j])
+        dv_ref[:, cols] = jnp.where(phase == 0, frecv[j], fsend[j])
 
 
 def body(n, nh, query, key_cache, value_cache, saved_output, out_grad, out_weight, doc_lengths):
@@ -349,7 +377,7 @@
     full = pl.BlockSpec(memory_space=pltpu.VMEM)
     anywhere = pl.BlockSpec(memory_space=pl.ANY)
     sizes = (n, nh, rows, kvh, groups, doc_lengths.shape[0], subs)
-    return pl.pallas_call(
+    results = pl.pallas_call(
         functools.partial(kernel, sizes),
         out_shape=(
             jax.ShapeDtypeStruct((1, rows, feats), f32),
@@ -383,21 +411,22 @@
             vmem((kvh, n, rows, HD), f32),
             vmem((kvh, n, rows, HD), bf),
             vmem((kvh, n, rows, HD), bf),
-            vmem((rows, kc), f32),
-            vmem((rows, kc), f32),
+            vmem((kvh, rows, HD), f32),
+            vmem((kvh, rows, HD), f32),
             dma((2 * ys * subs,)),
             dma((2,)),
             dma((2, n)), dma((2, n)), dma((2, n)), dma((2, n)),
             dma((ys * subs,)), dma((ys * subs,)),
             dma((others,)), dma((others,)),
             dma((kvh, n)), dma((kvh, n)), dma((kvh, n)), dma((kvh, n)),
-            dma(()), dma(()),
+            dma((kvh,)), dma((kvh,)),
         ],
         compiler_params=pltpu.CompilerParams(
             collective_id=0, has_side_effects=True, vmem_limit_bytes=60 * 2**20
         ),
         name="fused",
     )(query, key_cache, value_cache, saved_output, out_grad, out_weight[0], doc_lengths)
+    return results
 
 
 def solution(mesh):

time: 57.6 us -> 54.3 us (0.943)
  Pallas kernels: 52.9 us -> 49.5 us
    pallas_call x1, Pallas kernels: 52.9 us -> 49.5 us  [body(): pl.pallas_call(functools.partial(kernel, sizes), out_shape=(jax.ShapeDtyp...]
where the time goes in v1:
time: 54.3 us; the launch traced here: 54.1 us
  Pallas kernels  49.5 us (91%)
  local copies, waits for them, and re-layouts  3.93 us (7%)
  between operations  0.66 us (1%)
    pallas_call x1, Pallas kernels, body(): pl.pallas_call(functools.partial(kernel, sizes), out_shape=(jax.ShapeDtyp...  49.5 us
    unnamed x7, local copies, waits for them, and re-layouts  3.93 us

profile of v1, /device:TPU:0, one launch (start us, length us, event | category | flops | bytes accessed | tf_op | source)
XLA Modules:
  0.0 54.1 jit_solution(17180380053398060406)
XLA Ops:
  0.6 49.5 %fused.1 = (f32[1,256,1280]{2,1,0:T(8,128)}, f32[256,256]{1,0:T(8,128)}, f32[256,256]{1,0:T(8,128)}) custom-call(bf16[1,256,1280]{2,1,0:T(8,128)(2,1)} %query_ref.1, bf16[256,256]{1,0:T(8,128)(2,1)} %key_ref.1, bf16[256,256]{1,0:T(8,128)(2,1)} %value_ref.1, bf16[1,256,1280]{2,1,0:T(8,128)(2,1)} %saved_ref.1, bf16[1,256,1280]{2,1,0:T(8,128)(2,1)} %grad_ref.1, ...), custom_call_target="tpu_custom_call" | custom-call | tf_op jit(solution)/shard_map/fused/pallas_call | solution.py:380
  50.2 0.0 copy-start.1
  50.2 0.0 copy-start
  50.2 2.5 %copy.13 = f32[1,256,1280]{2,1,0:T(8,128)} copy(f32[1,256,1280]{2,1,0:T(8,128)} %get-tuple-element.6) | data formatting | bytes 2621440
  52.7 0.0 copy-done.1
  52.7 0.7 %copy.14 = f32[256,256]{1,0:T(8,128)} copy(f32[256,256]{1,0:T(8,128)S(1)} %copy-done.1) | data formatting | bytes 524288
  53.4 0.0 copy-done
  53.4 0.7 %copy.15 = f32[256,256]{1,0:T(8,128)} copy(f32[256,256]{1,0:T(8,128)S(1)} %copy-done) | data formatting | bytes 524288
Async XLA Ops:
  50.2 2.5 %copy-start.1 = (f32[256,256]{1,0:T(8,128)S(1)}, f32[256,256]{1,0:T(8,128)}, u32[]{:S(2)}) copy-start(f32[256,256]{1,0:T(8,128)} %get-tuple-element.7) | copy-start | bytes 786436
  50.2 3.2 %copy-start = (f32[256,256]{1,0:T(8,128)S(1)}, f32[256,256]{1,0:T(8,128)}, u32[]{:S(2)}) copy-start(f32[256,256]{1,0:T(8,128)} %get-tuple-element.8) | copy-start | bytes 786436
